TPU v7x, 1024 devices: a whole 8x8x8 slice. The times are simulated.
1024 devices in a mesh: scen: 128 (over x, y, core), arc: 8 (over z).
Axes of the slice: x: 8, y: 8, z: 8, core: 2. Of those that a mesh axis runs over, the one named last changes fastest.
Arguments:
- coupling: bfloat16 [1024, 4096], P(None, 'arc'), may hold values from -0.09375 to 0.09375
- incidence: int32 [8, 32], P(None, 'arc'), may hold values 0 or 1
- arc_cost: float32 [4096], P('arc'), may hold values from -6 to 6
- capacity: float32 [4096], P('arc'), may hold values from 0.5 to 2
- demand: float32 [128, 1024], P('scen'), may hold values from -4 to 4
- weights: int32 [128], P('scen'), may hold values from 128 to 24448, as said below
- fleet_slots: int32 [1024], P('arc'), may hold values from 0 to 511, as said below
Outputs:
- flows: float32 [128, 4096], P('scen', 'arc')
- duals: float32 [128, 1024], P('scen', 'arc')
- multipliers: float32 [128, 1024], P('scen', 'arc')
- consensus: float32 [1024], P('arc')
- spread: float32 [2], replicated
Inputs may be any that keep to these rules, and one draw needn't show every extreme that they name: `weights`: weight s is (128 + 2 s) times a power of two from 1 to 64. `fleet_slots`: within each aligned block of 128 entries (one arc block) the values are distinct positions inside that arc block.
All inputs are finite; a program needn't handle non-finite values. No bound on the sum of `incidence` on one device may be relied on, other than what follows from the above.
Results may differ from a plain program's by a relative error of at most 0.012.
Values may be sent and summed in bfloat16 or wider, within the bound.
A program may use at most 32 MiB of HBM per device.

v0:
```python
import jax
import jax.numpy as jnp
from jax import lax
from jax.sharding import PartitionSpec as P

TILE = 128
ITERS = 4
ROUNDS = 2


primal_step = 0.9
dual_step = 0.9
penalty = 1.0


def weighted_total(value):
    return lax.psum(value, "scen")


def body(coupling, incidence, arc_cost, capacity, demand, weights, fleet_slots):
    total_rows, block_arcs = coupling.shape
    masked = (
        coupling.reshape(total_rows // TILE, TILE, block_arcs // TILE, TILE)
        * incidence.astype(jnp.bfloat16)[:, None, :, None]
    ).reshape(total_rows, block_arcs)
    blocks = lax.axis_size("arc")
    share_rows = total_rows // blocks
    first_row = lax.axis_index("arc") * share_rows
    demand_row = demand[0]
    own_demand = lax.dynamic_slice_in_dim(demand_row, first_row, share_rows, 0)
    shares = weights.astype(jnp.float32)[0]
    fleet_count = fleet_slots.shape[0] * blocks
    weight_sum = jnp.float32(1.0)
    weight_sum = lax.psum(shares, "scen")
    flows = jnp.zeros((block_arcs,), jnp.float32)
    duals = jnp.zeros((share_rows,), jnp.float32)
    multipliers = jnp.zeros(fleet_slots.shape, jnp.float32)
    consensus = jnp.zeros(fleet_slots.shape, jnp.float32)
    spreads = []
    for round_index in range(ROUNDS):
        for step_index in range(ITERS):
            dual_full = lax.all_gather(duals.astype(jnp.bfloat16), "arc", axis=0, tiled=True)
            dual_pull = jnp.dot(dual_full, masked, preferred_element_type=jnp.float32)
            fleet_push = multipliers + penalty * (flows[fleet_slots] - consensus)
            gradient = (arc_cost + dual_pull).at[fleet_slots].add(fleet_push)
            flows_next = jnp.clip(flows - primal_step * gradient, 0.0, capacity)
            flows_bar = (2.0 * flows_next - flows).astype(jnp.bfloat16)
            row_load = lax.psum_scatter(
                jnp.dot(masked, flows_bar, preferred_element_type=jnp.float32),
                "arc",
                scatter_dimension=0,
                tiled=True,
            )
            duals = jnp.maximum(duals + dual_step * (row_load - own_demand), 0.0)
            flows = flows_next
        fleet_flow = flows[fleet_slots]
        weighted = weighted_total(shares * fleet_flow)
        consensus = weighted / weight_sum
        deviation = fleet_flow - consensus
        local_square = shares * jnp.sum(deviation * deviation)
        square_sum = lax.psum(local_square, ("scen", "arc"))
        spreads.append(jnp.sqrt(square_sum / (weight_sum * fleet_count) + 1e-06))
        multipliers = multipliers + penalty * deviation
    return (flows[None, :], duals[None, :], multipliers[None, :], consensus, jnp.stack(spreads))


def solution(mesh):
    in_specs = (
        P(None, "arc"),
        P(None, "arc"),
        P("arc"),
        P("arc"),
        P("scen", None),
        P("scen"),
        P("arc"),
    )
    out_specs = (P("scen", "arc"), P("scen", "arc"), P("scen", "arc"), P("arc"), P())
    return jax.shard_map(body, mesh=mesh, in_specs=in_specs, out_specs=out_specs, check_vma=False)
```

profile of v0, /device:TPU:1, one launch (start us, length us, event | category | flops | bytes accessed | tf_op | source)
XLA Modules:
  0.0 884.2 jit_solution(1016799128527511519)
XLA Ops:
  4.7 1.4 scatter_fusion
  6.5 26.6 %all-reduce = f32[1024]{0:T(1024)S(1)} all-reduce(f32[1024]{0:T(1024)S(1)} %bitcast.126), channel_id=2, replica_groups=mesh['scen'=128,'arc'=8] {'arc'}, use_global_device_ids=true, to_apply=%region_1.0.clone | all-reduce | flops 1024 | bytes 8192
  35.8 9.7 %all-gather = bf16[8,1,128]{2,1,0:T(2,128)(2,1)S(1)} all-gather(bf16[1,1,128]{2,1,0:T(2,128)(2,1)S(1)} %get-tuple-element.40), channel_id=1, replica_groups=mesh['scen'=128,'arc'=8] {'arc'}, dimensions={0}, use_global_device_ids=true | all-gather | bytes 2304 | tf_op jit(solution)/shard_map/all_gather | solution.py:42
  45.7 1.3 gather_fusion.1
  47.0 1.4 scatter_fusion.1
  48.9 12.1 %all-reduce.1 = f32[1024]{0:T(1024)S(1)} all-reduce(f32[1024]{0:T(1024)S(1)} %bitcast.127), channel_id=3, replica_groups=mesh['scen'=128,'arc'=8] {'arc'}, use_global_device_ids=true, to_apply=%region_3.4.clone | all-reduce | flops 1024 | bytes 8192
  61.1 9.7 %all-gather.1 = bf16[8,1,128]{2,1,0:T(2,128)(2,1)S(1)} all-gather(bf16[1,1,128]{2,1,0:T(2,128)(2,1)S(1)} %get-tuple-element.36), channel_id=1, replica_groups=mesh['scen'=128,'arc'=8] {'arc'}, dimensions={0}, use_global_device_ids=true | all-gather | bytes 2304 | tf_op jit(solution)/shard_map/all_gather | solution.py:42
  71.0 1.3 gather_fusion.2
  72.3 1.4 scatter_fusion.2
  74.1 12.1 %all-reduce.2 = f32[1024]{0:T(1024)S(1)} all-reduce(f32[1024]{0:T(1024)S(1)} %bitcast.128), channel_id=4, replica_groups=mesh['scen'=128,'arc'=8] {'arc'}, use_global_device_ids=true, to_apply=%region_5.6.clone | all-reduce | flops 1024 | bytes 8192
  86.3 9.7 %all-gather.2 = bf16[8,1,128]{2,1,0:T(2,128)(2,1)S(1)} all-gather(bf16[1,1,128]{2,1,0:T(2,128)(2,1)S(1)} %get-tuple-element.32), channel_id=1, replica_groups=mesh['scen'=128,'arc'=8] {'arc'}, dimensions={0}, use_global_device_ids=true | all-gather | bytes 2304 | tf_op jit(solution)/shard_map/all_gather | solution.py:42
  96.3 1.3 gather_fusion.3
  97.5 1.4 scatter_fusion.3
  99.4 12.3 %all-reduce.3 = f32[1024]{0:T(1024)S(1)} all-reduce(f32[1024]{0:T(1024)S(1)} %bitcast.129), channel_id=5, replica_groups=mesh['scen'=128,'arc'=8] {'arc'}, use_global_device_ids=true, to_apply=%region_7.8.clone | all-reduce | flops 1024 | bytes 8192
  111.7 9.7 %all-gather.3 = bf16[8,1,128]{2,1,0:T(2,128)(2,1)S(1)} all-gather(bf16[1,1,128]{2,1,0:T(2,128)(2,1)S(1)} %get-tuple-element.28), channel_id=1, replica_groups=mesh['scen'=128,'arc'=8] {'arc'}, dimensions={0}, use_global_device_ids=true | all-gather | bytes 2304 | tf_op jit(solution)/shard_map/all_gather | solution.py:42
  121.7 1.3 gather_fusion.4
  123.6 279.2 %all-reduce.9 = (f32[128]{0:T(128)S(1)}, f32[]{:T(128)}) all-reduce(f32[128]{0:T(128)S(1)} %broadcast_multiply_fusion.1, f32[]{:T(128)} %bitcast.14), channel_id=1, replica_groups=mesh['scen'=128,'arc'=8] {'scen'}, use_global_device_ids=true, to_apply=%region_8.9 | all-reduce | flops 129 | bytes 1032 | tf_op jit(solution)/shard_map/psum | solution.py:17
  402.9 1.3 multiply_reduce_fusion.1
  404.1 1.4 scatter_fusion.4
  406.0 12.4 %all-reduce.4 = f32[1024]{0:T(1024)S(1)} all-reduce(f32[1024]{0:T(1024)S(1)} %bitcast.130), channel_id=6, replica_groups=mesh['scen'=128,'arc'=8] {'arc'}, use_global_device_ids=true, to_apply=%region_11.12.clone | all-reduce | flops 1024 | bytes 8192
  418.5 9.7 %all-gather.4 = bf16[8,1,128]{2,1,0:T(2,128)(2,1)S(1)} all-gather(bf16[1,1,128]{2,1,0:T(2,128)(2,1)S(1)} %get-tuple-element.24), channel_id=1, replica_groups=mesh['scen'=128,'arc'=8] {'arc'}, dimensions={0}, use_global_device_ids=true | all-gather | bytes 2304 | tf_op jit(solution)/shard_map/all_gather | solution.py:42
  429.7 1.4 scatter_fusion.5
  431.5 12.1 %all-reduce.5 = f32[1024]{0:T(1024)S(1)} all-reduce(f32[1024]{0:T(1024)S(1)} %bitcast.131), channel_id=7, replica_groups=mesh['scen'=128,'arc'=8] {'arc'}, use_global_device_ids=true, to_apply=%region_13.14.clone | all-reduce | flops 1024 | bytes 8192
  443.7 10.0 %all-gather.5 = bf16[8,1,128]{2,1,0:T(2,128)(2,1)S(1)} all-gather(bf16[1,1,128]{2,1,0:T(2,128)(2,1)S(1)} %get-tuple-element.20), channel_id=1, replica_groups=mesh['scen'=128,'arc'=8] {'arc'}, dimensions={0}, use_global_device_ids=true | all-gather | bytes 2304 | tf_op jit(solution)/shard_map/all_gather | solution.py:42
  455.2 1.4 scatter_fusion.6
  457.1 12.1 %all-reduce.6 = f32[1024]{0:T(1024)S(1)} all-reduce(f32[1024]{0:T(1024)S(1)} %bitcast.132), channel_id=8, replica_groups=mesh['scen'=128,'arc'=8] {'arc'}, use_global_device_ids=true, to_apply=%region_15.16.clone | all-reduce | flops 1024 | bytes 8192
  469.3 9.9 %all-gather.6 = bf16[8,1,128]{2,1,0:T(2,128)(2,1)S(1)} all-gather(bf16[1,1,128]{2,1,0:T(2,128)(2,1)S(1)} %get-tuple-element.16), channel_id=1, replica_groups=mesh['scen'=128,'arc'=8] {'arc'}, dimensions={0}, use_global_device_ids=true | all-gather | bytes 2304 | tf_op jit(solution)/shard_map/all_gather | solution.py:42
  480.7 1.4 scatter_fusion.7
  482.6 12.2 %all-reduce.7 = f32[1024]{0:T(1024)S(1)} all-reduce(f32[1024]{0:T(1024)S(1)} %bitcast.125), channel_id=9, replica_groups=mesh['scen'=128,'arc'=8] {'arc'}, use_global_device_ids=true, to_apply=%region_17.18.clone | all-reduce | flops 1024 | bytes 8192
  496.7 272.2 %psum.37 = f32[128]{0:T(128)S(1)} all-reduce(f32[128]{0:T(128)S(1)} %broadcast_multiply_fusion), channel_id=1, replica_groups=mesh['scen'=128,'arc'=8] {'scen'}, use_global_device_ids=true, to_apply=%region_18.19 | all-reduce | flops 128 | bytes 1024 | tf_op jit(solution)/shard_map/psum | solution.py:17
  768.9 1.3 multiply_reduce_fusion
  772.4 109.2 %all-reduce.8 = (f32[]{:T(128)}, f32[]{:T(128)}) all-reduce(f32[]{:T(128)S(6)} %mul.147, f32[]{:T(128)S(6)} %mul.144), channel_id=1, replica_groups=mesh['scen'=128,'arc'=8] {'scen','arc'}, use_global_device_ids=true, to_apply=%region_22.23 | all-reduce | flops 2 | bytes 16 | tf_op jit(solution)/shard_map/psum | solution.py:61
  (81 shorter events, 18.6 us)
Async XLA Ops:
  0.6 1.2 copy-start.1
  2.0 0.7 copy-start.2
  2.7 0.7 copy-start.5
  4.7 1.4 copy-start.3
  482.2 13.2 %copy-start = (f32[512]{0:T(512)}, f32[512]{0:T(512)S(1)}, u32[]{:S(2)}) copy-start(f32[512]{0:T(512)S(1)} %get-tuple-element.15) | copy-start | bytes 6148
  770.2 0.5 copy-start.4
where the time goes:
time: 885 us; the launch traced here: 884 us
  blocking collectives  841 us (95%)
  other arithmetic  18.1 us (2%)
  local copies, waits for them, and re-layouts  14.9 us (2%)
    psum x2, blocking collectives, weighted_total(): return lax.psum(value, 'scen')  551 us
    unnamed x8, blocking collectives  112 us
    psum x1, blocking collectives, body(): square_sum = lax.psum(local_square, ('scen', 'arc'))  109 us
    all_gather x7, blocking collectives, body(): lax.all_gather(duals.astype(jnp.bfloat16), 'arc', axis=0, tiled=True)  68.4 us

commit v1 on v0

v1 whole, which is shorter than its diff:
```python
import functools

import jax
import jax.numpy as jnp
from jax import lax
from jax.experimental import pallas as pl
from jax.experimental.pallas import tpu as pltpu
from jax.sharding import PartitionSpec as P

TILE = 128
ITERS = 4
ROUNDS = 2

primal_step = 0.9
dual_step = 0.9
penalty = 1.0

MESH = pl.DeviceIdType.MESH
NX, NY, NC = 8, 8, 2
NZ = 8
NG = NX * NC
NN = (((1,), (0,)), ((), ()))
NT = (((1,), (1,)), ((), ()))


def dot(left, right, dims):
    return lax.dot_general(left, right, dims, preferred_element_type=jnp.float32)


def thirds(value):
    high = value.astype(jnp.bfloat16).astype(jnp.float32)
    rest = value - high
    middle = rest.astype(jnp.bfloat16).astype(jnp.float32)
    low = rest - middle
    return jnp.concatenate([high, middle, low], axis=0).astype(jnp.bfloat16)


def joined(rows):
    return (rows[0:1] + rows[1:2]) + rows[2:3]


def kernel(
    incidence,
    weights,
    coupling,
    cost_ref,
    capacity_ref,
    demand_ref,
    slots_ref,
    flows_out,
    duals_out,
    multipliers_out,
    consensus_out,
    spread_out,
    masked,
    pick,
    loads,
    group,
    plane,
    squares,
    duals_ref,
    copy_sem,
    load_send,
    load_recv,
    group_send,
    group_recv,
    plane_send,
    plane_recv,
    square_send,
    square_recv,
):
    scen = lax.axis_index("scen")
    z = lax.axis_index("arc")
    x = scen // (NY * NC)
    y = (scen // NC) % NY
    core = scen % NC
    mine = x * NC + core

    def z_partner(step):
        return (scen, lax.rem(z + step, NZ))

    def group_partner(step):
        other = lax.rem(mine + step, NG)
        return ((other // NC * NY + y) * NC + other % NC, z)

    def plane_partner(step):
        return ((x * NY + lax.rem(y + step, NY)) * NC + core, z)

    barrier = pltpu.get_barrier_semaphore()
    for step in range(1, NZ):
        pl.semaphore_signal(barrier, inc=1, device_id=z_partner(step), device_id_type=MESH)
    for step in range(1, NG):
        pl.semaphore_signal(barrier, inc=1, device_id=group_partner(step), device_id_type=MESH)
    for step in range(1, NY):
        pl.semaphore_signal(barrier, inc=1, device_id=plane_partner(step), device_id_type=MESH)

    blocks = coupling.shape[0] // TILE
    arcs = coupling.shape[1]
    fetch = pltpu.make_async_copy(coupling, masked, copy_sem)
    fetch.start()

    cost = cost_ref[...]
    capacity = capacity_ref[...]
    demand = demand_ref[...]
    slots = slots_ref[...]
    fleets = slots.shape[1]
    places = lax.broadcasted_iota(jnp.int32, (arcs, fleets), 0)
    pick[...] = jnp.where(places == slots, 1.0, 0.0).astype(jnp.bfloat16)
    is_fleet = dot(jnp.ones((1, fleets), jnp.bfloat16), pick[...], NT) > 0.5
    share = jnp.full((1, fleets), weights[0].astype(jnp.float32))

    fetch.wait()
    for row in range(blocks):
        for column in range(arcs // TILE):
            tile = (pl.ds(row * TILE, TILE), pl.ds(column * TILE, TILE))
            factor = incidence[row, column].astype(jnp.float32)
            masked[tile] = masked[tile] * jnp.full((TILE, TILE), factor, jnp.float32).astype(jnp.bfloat16)

    def send_all(buffer, own, partner, count, send_sem, recv_sem):
        for step in range(1, count):
            pltpu.make_async_remote_copy(
                src_ref=buffer.at[own],
                dst_ref=buffer.at[own],
                send_sem=send_sem,
                recv_sem=recv_sem,
                device_id=partner(step),
                device_id_type=MESH,
            ).start()

    def others(buffer, partner, count, send_sem, recv_sem):
        rest = buffer.at[pl.ds(0, count - 1)]
        return pltpu.make_async_remote_copy(
            src_ref=rest,
            dst_ref=rest,
            send_sem=send_sem,
            recv_sem=recv_sem,
            device_id=partner(1),
            device_id_type=MESH,
        )

    flows = jnp.zeros((1, arcs), jnp.float32)
    duals = jnp.zeros(demand.shape, jnp.float32)
    multipliers = jnp.zeros((1, fleets), jnp.float32)
    arc_multipliers = jnp.zeros((1, arcs), jnp.float32)
    arc_consensus = jnp.zeros((1, arcs), jnp.float32)
    pending = []
    deviations = []
    for round_index in range(ROUNDS):
        for step_index in range(ITERS):
            turn = round_index * ITERS + step_index
            gradient = cost
            if turn > 0:
                row = jnp.concatenate([duals[i : i + 1] for i in range(blocks)], axis=1)
                gradient = cost + dot(row.astype(jnp.bfloat16), masked[...], NN)
                if step_index == 0:
                    last = round_index - 1
                    wait = others(plane.at[last], plane_partner, NY, plane_send.at[last], plane_recv.at[last])
                    wait.wait_recv()
                    pending.append(wait)
                    consensus, weight_sum, square = settle(plane.at[last])
                    deviations.append(square)
                    multipliers = multipliers + penalty * (fleet_flow - consensus)
                    arc_consensus = joined(dot(thirds(consensus), pick[...], NT))
                    arc_multipliers = arc_multipliers + penalty * jnp.where(is_fleet, flows - arc_consensus, 0.0)
                push = arc_multipliers + penalty * (flows - arc_consensus)
                gradient = gradient + jnp.where(is_fleet, push, 0.0)
            flows_next = jnp.clip(flows - primal_step * gradient, 0.0, capacity)
            flows_bar = (2.0 * flows_next - flows).astype(jnp.bfloat16)
            flows = flows_next
            if turn == 0:
                pl.semaphore_wait(barrier, NZ + NG + NY - 3)
            if step_index == ITERS - 1:
                fleet_flow = joined(dot(thirds(flows), pick[...], NN))
                heap = group.at[round_index]
                heap[mine] = jnp.concatenate([fleet_flow, share], axis=0)
                send_all(heap, mine, group_partner, NG, group_send.at[round_index], group_recv.at[round_index])
            load = dot(flows_bar, masked[...], NT)
            heap = loads.at[turn]
            for i in range(blocks):
                heap[z, i : i + 1, :] = load[:, i * TILE : (i + 1) * TILE]
            send_all(heap, z, z_partner, NZ, load_send.at[turn], load_recv.at[turn])
            if step_index == ITERS - 1:
                heap = group.at[round_index]
                wait = others(heap, group_partner, NG, group_send.at[round_index], group_recv.at[round_index])
                wait.wait_recv()
                pending.append(wait)
                total = jnp.zeros((1, fleets), jnp.float32)
                weight = jnp.zeros((1, fleets), jnp.float32)
                for i in range(NG):
                    total = total + heap[i, 1:2] * heap[i, 0:1]
                    weight = weight + heap[i, 1:2]
                mean = total / weight
                square = jnp.zeros((1, fleets), jnp.float32)
                for i in range(NG):
                    gap = heap[i, 0:1] - mean
                    square = square + heap[i, 1:2] * gap * gap
                heap = plane.at[round_index]
                heap[y] = jnp.concatenate([total, weight, mean, square], axis=0)
                send_all(heap, y, plane_partner, NY, plane_send.at[round_index], plane_recv.at[round_index])
            heap = loads.at[turn]
            wait = others(heap, z_partner, NZ, load_send.at[turn], load_recv.at[turn])
            wait.wait_recv()
            pending.append(wait)
            row_load = heap[0]
            for i in range(1, NZ):
                row_load = row_load + heap[i]
            duals = jnp.maximum(duals + dual_step * (row_load - demand), 0.0)

    flows_out[...] = flows
    duals_ref[...] = duals
    duals_out[...] = duals_ref[pl.ds(z, 1), :]

    last = ROUNDS - 1
    wait = others(plane.at[last], plane_partner, NY, plane_send.at[last], plane_recv.at[last])
    wait.wait_recv()
    pending.append(wait)
    consensus, weight_sum, square = settle(plane.at[last])
    deviations.append(square)
    squares[z] = jnp.concatenate(deviations, axis=0)
    send_all(squares, z, z_partner, NZ, square_send, square_recv)
    consensus_out[...] = consensus
    multipliers_out[...] = multipliers + penalty * (fleet_flow - consensus)
    wait = others(squares, z_partner, NZ, square_send, square_recv)
    wait.wait_recv()
    pending.append(wait)
    total = squares[0]
    for i in range(1, NZ):
        total = total + squares[i]
    total = jnp.sum(total, axis=1, keepdims=True)
    spread_out[...] = jnp.sqrt(total / (weight_sum[:, 0:1] * (fleets * NZ)) + 1e-06)
    for wait in pending:
        wait.wait_send()


def settle(heap):
    total = heap[0, 0:1]
    weight = heap[0, 1:2]
    for i in range(1, NY):
        total = total + heap[i, 0:1]
        weight = weight + heap[i, 1:2]
    consensus = total / weight
    square = jnp.zeros_like(total)
    for i in range(NY):
        gap = heap[i, 2:3] - consensus
        square = square + (heap[i, 3:4] + heap[i, 1:2] * gap * gap)
    return consensus, weight, square


def body(coupling, incidence, arc_cost, capacity, demand, weights, fleet_slots):
    rows, arcs = coupling.shape
    fleets = fleet_slots.shape[0]
    turns = ROUNDS * ITERS
    f32 = jnp.float32
    vmem = pl.BlockSpec(memory_space=pltpu.VMEM)
    smem = pl.BlockSpec(memory_space=pltpu.SMEM)
    flows, duals, multipliers, consensus, spread = pl.pallas_call(
        kernel,
        out_shape=[
            jax.ShapeDtypeStruct((1, arcs), f32),
            jax.ShapeDtypeStruct((1, rows // NZ), f32),
            jax.ShapeDtypeStruct((1, fleets), f32),
            jax.ShapeDtypeStruct((1, fleets), f32),
            jax.ShapeDtypeStruct((ROUNDS, 1), f32),
        ],
        in_specs=[smem, smem, pl.BlockSpec(memory_space=pl.ANY)] + [vmem] * 4,
        out_specs=[vmem] * 5,
        scratch_shapes=[
            pltpu.VMEM((rows, arcs), jnp.bfloat16),
            pltpu.VMEM((arcs, fleets), jnp.bfloat16),
            pltpu.VMEM((turns, NZ, rows // TILE, TILE), f32),
            pltpu.VMEM((ROUNDS, NG, 2, fleets), f32),
            pltpu.VMEM((ROUNDS, NY, 4, fleets), f32),
            pltpu.VMEM((NZ, ROUNDS, fleets), f32),
            pltpu.VMEM((rows // TILE, TILE), f32),
            pltpu.SemaphoreType.DMA,
            pltpu.SemaphoreType.DMA((turns,)),
            pltpu.SemaphoreType.DMA((turns,)),
            pltpu.SemaphoreType.DMA((ROUNDS,)),
            pltpu.SemaphoreType.DMA((ROUNDS,)),
            pltpu.SemaphoreType.DMA((ROUNDS,)),
            pltpu.SemaphoreType.DMA((ROUNDS,)),
            pltpu.SemaphoreType.DMA,
            pltpu.SemaphoreType.DMA,
        ],
        compiler_params=pltpu.CompilerParams(
            collective_id=0, has_side_effects=True, vmem_limit_bytes=16 * 1024 * 1024
        ),
        cost_estimate=pl.CostEstimate(
            flops=4 * turns * rows * arcs, bytes_accessed=2 * rows * arcs, transcendentals=0
        ),
    )(
        incidence,
        weights,
        coupling,
        arc_cost.reshape(1, arcs),
        capacity.reshape(1, arcs),
        demand.reshape(rows // TILE, TILE),
        fleet_slots.reshape(1, fleets),
    )
    return flows, duals, multipliers, consensus.reshape(fleets), spread.reshape(ROUNDS)


def solution(mesh):
    in_specs = (
        P(None, "arc"),
        P(None, "arc"),
        P("arc"),
        P("arc"),
        P("scen", None),
        P("scen"),
        P("arc"),
    )
    out_specs = (P("scen", "arc"), P("scen", "arc"), P("scen", "arc"), P("arc"), P())
    return jax.shard_map(body, mesh=mesh, in_specs=in_specs, out_specs=out_specs, check_vma=False)
```

time: 885 us -> 84 us (0.09)
  blocking collectives: 841 us -> 0 us
  Pallas kernels: 0 us -> 77.1 us
  other arithmetic: 18.1 us -> 0.63 us
  local copies, waits for them, and re-layouts: 14.9 us -> 4.67 us
    psum x3 -> x0, blocking collectives: 661 us -> none  [the longest x2 551 us: weighted_total(): return lax.psum(value, 'scen')]
    unnamed x8 -> x0, blocking collectives: 112 us -> none
    pallas_call x0 -> x1, Pallas kernels: none -> 77.1 us  [body(): pl.pallas_call(kernel, out_shape=[jax.ShapeDtypeStruct((1, arcs), f32), j...]
    all_gather x7 -> x0, blocking collectives: 68.4 us -> none  [body(): lax.all_gather(duals.astype(jnp.bfloat16), 'arc', axis=0, tiled=True)]
    gather x9 -> x0, local copies, waits for them, and re-layouts: 11.5 us -> none  [the longest x7 8.94 us: body(): fleet_push = multipliers + penalty * (flows[fleet_slots] - consensus)]
    scatter-add x8 -> x0, other arithmetic: 11.4 us -> none  [body(): gradient = (arc_cost + dual_pull).at[fleet_slots].add(fleet_push)]
where the time goes in v1:
time: 84 us; the launch traced here: 83.8 us
  Pallas kernels  77.1 us (92%)
  local copies, waits for them, and re-layouts  4.67 us (6%)
  between operations  1.32 us (2%)
    pallas_call x1, Pallas kernels, body(): pl.pallas_call(kernel, out_shape=[jax.ShapeDtypeStruct((1, arcs), f32), j...  77.1 us
    unnamed x17, local copies, waits for them, and re-layouts  4.67 us

profile of v1, /device:TPU:1, one launch (start us, length us, event | category | flops | bytes accessed | tf_op | source)
XLA Modules:
  0.0 83.8 jit_solution(2345099031280291591)
XLA Ops:
  1.3 0.0 copy-start.5
  1.3 0.0 copy-start.3
  1.3 0.0 copy-start.1
  1.3 0.7 copy-done.5
  2.0 0.0 copy-start.2
  2.0 0.0 copy-start.4
  2.0 0.1 copy.13.incidence
  2.0 0.0 copy-done.3
  2.1 0.0 copy-done.1
  2.1 0.6 copy-done.2
  2.6 0.0 copy-done.4
  2.6 0.0 copy-start
  2.6 1.2 %copy-done = bf16[1024,512]{1,0:T(8,128)(2,1)S(1)} copy-done((bf16[1024,512]{1,0:T(8,128)(2,1)S(1)}, bf16[1024,512]{1,0:T(8,128)(2,1)}, u32[]{:S(2)}) %copy-start) | copy-done | bytes 1048600
  3.9 77.1 %shard_map.110 = (f32[1,512]{1,0:T(1,128)S(1)}, f32[1,128]{1,0:T(1,128)S(1)}, f32[1,128]{1,0:T(1,128)S(1)}, f32[1,128]{1,0:T(1,128)S(1)}, f32[2,1]{1,0:T(2,128)S(1)}) custom-call(s32[8,4]{1,0:T(8,128)S(1)} %copy.13.incidence, s32[1]{0:T(128)S(6)} %copy.18.weights, bf16[1024,512]{1,0:T(8,128)(2,1)S(1)} %copy-done, f32[1,512]{1,0:T(1,128)S(1)} %bitcast.6, ...), custom_call_target="tpu_custom_call" | custom-call | flops 16777216 | bytes 1048576 | tf_op jit(solution)/shard_map/pallas_call | solution.py:256
  81.0 0.6 reduce
  81.6 0.6 copy.19
  82.2 0.5 copy.20
  82.7 0.5 copy.21
  83.2 0.5 copy.22
Async XLA Ops:
  1.3 0.7 copy-start.5
  1.3 0.8 copy-start.3
  1.3 0.8 copy-start.1
  2.0 0.7 copy-start.2
  2.0 0.7 copy-start.4
  2.6 1.2 %copy-start = (bf16[1024,512]{1,0:T(8,128)(2,1)S(1)}, bf16[1024,512]{1,0:T(8,128)(2,1)}, u32[]{:S(2)}) copy-start(bf16[1024,512]{1,0:T(8,128)(2,1)} %coupling.1) | copy-start | bytes 3145732

commit v2 on v0

v2 whole, which is shorter than its diff:
```python
import jax
import jax.numpy as jnp
from jax import lax
from jax.experimental import pallas as pl
from jax.experimental.pallas import tpu as pltpu
from jax.sharding import PartitionSpec as P

TILE = 128
ITERS = 4
ROUNDS = 2

primal_step = 0.9
dual_step = 0.9
penalty = 1.0

MESH = pl.DeviceIdType.MESH
NX, NY, NC, NZ = 8, 8, 2, 8
NG = NX * NC
SCEN = NG * NY
CHUNKS = 4
NN = (((1,), (0,)), ((), ()))
NT = (((1,), (1,)), ((), ()))


def dot(left, right, dims):
    return lax.dot_general(left, right, dims, preferred_element_type=jnp.float32)


def thirds(value):
    high = value.astype(jnp.bfloat16).astype(jnp.float32)
    rest = value - high
    middle = rest.astype(jnp.bfloat16).astype(jnp.float32)
    low = rest - middle
    return jnp.concatenate([high, middle, low], axis=0).astype(jnp.bfloat16)


def joined(rows):
    return (rows[0:1] + rows[1:2]) + rows[2:3]


def far(size):
    return sorted(range(size), key=lambda step: -min(step, size - step))


def hops(step, size):
    return min(step, size - step)


def kernel(
    coupling_hbm,
    incidence_hbm,
    cost_hbm,
    capacity_hbm,
    demand_hbm,
    weights_hbm,
    slots_hbm,
    flows_out,
    duals_out,
    multipliers_out,
    consensus_out,
    spread_out,
    flows_ref,
    duals_ref,
    multipliers_ref,
    consensus_ref,
    spread_ref,
    incidence,
    weights,
    cost_ref,
    capacity_ref,
    demand_ref,
    slots_ref,
    masked,
    turned,
    pick,
    loads,
    shares,
    fleet,
    squares,
    all_duals,
    fetch_sem,
    store_sem,
    load_send,
    load_recv,
    share_send,
    share_recv,
    fleet_send,
    fleet_recv,
    square_send,
    square_recv,
):
    scen = lax.axis_index("scen")
    z = lax.axis_index("arc")
    x = scen // (NY * NC)
    y = (scen // NC) % NY
    core = scen % NC
    mine = y * NG + x * NC + core

    def at(dx, dy, dc):
        other = (lax.rem(x + dx, NX) * NY + lax.rem(y + dy, NY)) * NC + lax.rem(core + dc, NC)
        return (other, z)

    along_z = [(scen, lax.rem(z + step, NZ)) for step in far(NZ)[:-1]]
    group = [at(dx, 0, dc) for dx in far(NX) for dc in (1, 0) if dx + dc > 0]
    plane = [at(0, dy, 0) for dy in far(NY)[:-1]]
    steps = [(dx, dy, dc) for dx in range(NX) for dy in range(NY) for dc in range(NC)]
    steps = [s for s in steps if s != (0, 0, 0)]
    steps.sort(key=lambda s: -hops(s[0], NX) - hops(s[1], NY))

    barrier = pltpu.get_barrier_semaphore()
    greeted = along_z + group + plane
    for other in greeted:
        pl.semaphore_signal(barrier, inc=1, device_id=other, device_id_type=MESH)

    rows, arcs = masked.shape
    blocks = rows // TILE
    fleets = slots_ref.shape[1]
    depth = rows // CHUNKS
    fetches = []

    def fetch(source, target):
        copy = pltpu.make_async_copy(source, target, fetch_sem.at[len(fetches)])
        copy.start()
        fetches.append(copy)
        return copy

    fetch_incidence = fetch(incidence_hbm, incidence)
    fetch_cost = fetch(cost_hbm, cost_ref)
    fetch_capacity = fetch(capacity_hbm, capacity_ref)
    parts = [pl.ds(chunk * depth, depth) for chunk in range(CHUNKS)]
    fetch_masked = [fetch(coupling_hbm.at[part], masked.at[part]) for part in parts]
    fetch_slots = fetch(slots_hbm, slots_ref)
    fetch_demand = fetch(demand_hbm, demand_ref)
    fetch_weights = fetch(weights_hbm, weights)

    def store(index, source, target):
        copy = pltpu.make_async_copy(source, target, store_sem.at[index])
        copy.start()
        return copy

    def send(source, target, partner, send_sem, recv_sem):
        pltpu.make_async_remote_copy(
            src_ref=source,
            dst_ref=target,
            send_sem=send_sem,
            recv_sem=recv_sem,
            device_id=partner,
            device_id_type=MESH,
        ).start()

    def awaited(rest, send_sem, recv_sem):
        return pltpu.make_async_remote_copy(
            src_ref=rest,
            dst_ref=rest,
            send_sem=send_sem,
            recv_sem=recv_sem,
            device_id=along_z[0],
            device_id_type=MESH,
        )

    def exchange(buffer, send_sem, recv_sem):
        for partner in along_z:
            send(buffer.at[z], buffer.at[z], partner, send_sem, recv_sem)
        return awaited(buffer.at[pl.ds(0, NZ - 1)], send_sem, recv_sem)

    fetch_cost.wait()
    fetch_capacity.wait()
    cost = cost_ref[...]
    capacity = capacity_ref[...]
    flows = jnp.clip(-primal_step * cost, 0.0, capacity)
    flows_bar = (2.0 * flows).astype(jnp.bfloat16)
    fetch_incidence.wait()
    for chunk, part in enumerate(parts):
        fetch_masked[chunk].wait()
        for row in range(chunk * depth // TILE, (chunk + 1) * depth // TILE):
            for column in range(arcs // TILE):
                tile = (pl.ds(row * TILE, TILE), pl.ds(column * TILE, TILE))
                factor = incidence[column, row].astype(jnp.float32)
                masked[tile] = masked[tile] * jnp.full((TILE, TILE), factor, jnp.float32).astype(jnp.bfloat16)
        load = dot(flows_bar, masked[part], NT)
        for i in range(depth // TILE):
            loads[0, z, pl.ds(chunk * depth // TILE + i, 1), :] = load[:, i * TILE : (i + 1) * TILE]
    pl.semaphore_wait(barrier, len(greeted))
    waits = [exchange(loads.at[0], load_send.at[0], load_recv.at[0])]

    fetch_weights.wait()
    own_row = pl.ds(mine, 1)
    shares[own_row, :] = jnp.full((1, fleets), weights[0].astype(jnp.float32))
    for partner in group:
        send(shares.at[own_row], shares.at[own_row], partner, share_send.at[0], share_recv.at[0])
    share_group = awaited(shares.at[pl.ds(0, NG - 1)], share_send.at[0], share_recv.at[0])
    for part in parts:
        turned[:, part] = masked[part].T
    fetch_slots.wait()
    places = lax.broadcasted_iota(jnp.int32, (arcs, fleets), 0)
    pick[...] = jnp.where(places == slots_ref[...], 1.0, 0.0).astype(jnp.bfloat16)
    is_fleet = dot(jnp.ones((1, fleets), jnp.bfloat16), pick[...], NT) > 0.5
    fetch_demand.wait()
    demand = demand_ref[...]

    def next_duals(duals, turn):
        waits[turn].wait_recv()
        row_load = loads[turn, 0]
        for i in range(1, NZ):
            row_load = row_load + loads[turn, i]
        return jnp.maximum(duals + dual_step * (row_load - demand), 0.0)

    duals = next_duals(jnp.zeros(demand.shape, jnp.float32), 0)
    multipliers = jnp.zeros((1, fleets), jnp.float32)
    arc_multipliers = jnp.zeros((1, arcs), jnp.float32)
    arc_consensus = jnp.zeros((1, arcs), jnp.float32)
    deviations = []
    pending = []
    for turn in range(1, ROUNDS * ITERS):
        row = jnp.concatenate([duals[i : i + 1] for i in range(blocks)], axis=1)
        gradient = cost + dot(row.astype(jnp.bfloat16), masked[...], NN)
        push = arc_multipliers + penalty * (flows - arc_consensus)
        gradient = gradient + jnp.where(is_fleet, push, 0.0)
        flows_next = jnp.clip(flows - primal_step * gradient, 0.0, capacity)
        flows_bar = (2.0 * flows_next - flows).astype(jnp.bfloat16)
        flows = flows_next
        round_index = turn // ITERS
        round_ends = turn % ITERS == ITERS - 1
        if round_ends:
            fleet_flow = joined(dot(thirds(flows), pick[...], NN))
            heap = fleet.at[round_index]
            fleet[round_index, own_row, :] = fleet_flow
            for step in steps:
                send(
                    heap.at[own_row],
                    heap.at[own_row],
                    at(*step),
                    fleet_send.at[round_index],
                    fleet_recv.at[round_index],
                )
            arrival = awaited(
                heap.at[pl.ds(0, SCEN - 1)], fleet_send.at[round_index], fleet_recv.at[round_index]
            )
        load = dot(flows_bar, turned[...], NN)
        for i in range(blocks):
            loads[turn, z, i : i + 1, :] = load[:, i * TILE : (i + 1) * TILE]
        waits.append(exchange(loads.at[turn], load_send.at[turn], load_recv.at[turn]))
        if turn == 1:
            share_group.wait_recv()
            own_rows = pl.ds(pl.multiple_of(y * NG, NG), NG)
            for partner in plane:
                send(shares.at[own_rows], shares.at[own_rows], partner, share_send.at[1], share_recv.at[1])
            share_plane = awaited(shares.at[pl.ds(0, SCEN - NG)], share_send.at[1], share_recv.at[1])
        if turn == 2:
            share_plane.wait_recv()
            pending += [share_group, share_plane]
            weight_sum = jnp.sum(shares[...], axis=0, keepdims=True)
        duals = next_duals(duals, turn)
        if round_ends:
            if turn == ROUNDS * ITERS - 1:
                flows_ref[...] = flows
                all_duals[...] = duals
                duals_ref[...] = all_duals[pl.ds(z, 1), :]
                stores = [store(0, flows_ref, flows_out), store(1, duals_ref, duals_out)]
            arrival.wait_recv()
            pending.append(arrival)
            all_fleet = heap[...]
            consensus = jnp.sum(shares[...] * all_fleet, axis=0, keepdims=True) / weight_sum
            gap = all_fleet - consensus
            deviations.append(jnp.sum(shares[...] * gap * gap, axis=0, keepdims=True))
            multipliers = multipliers + penalty * (fleet_flow - consensus)
            if turn < ROUNDS * ITERS - 1:
                arc_consensus = joined(dot(thirds(consensus), pick[...], NT))
                arc_multipliers = arc_multipliers + penalty * jnp.where(is_fleet, flows - arc_consensus, 0.0)

    squares[z] = jnp.concatenate(deviations, axis=0)
    wait = exchange(squares, square_send, square_recv)
    multipliers_ref[...] = multipliers
    consensus_ref[...] = consensus
    stores += [store(2, multipliers_ref, multipliers_out), store(3, consensus_ref, consensus_out)]
    for done in waits + pending:
        done.wait_send()
    wait.wait_recv()
    total = squares[0]
    for i in range(1, NZ):
        total = total + squares[i]
    total = jnp.sum(total, axis=1, keepdims=True)
    spread = jnp.sqrt(total / (weight_sum[:, 0:1] * (fleets * NZ)) + 1e-06)
    spread_ref[...] = jnp.concatenate([spread[i : i + 1] for i in range(ROUNDS)], axis=1)
    stores.append(store(4, spread_ref, spread_out))
    wait.wait_send()
    for done in stores:
        done.wait()


def place(*refs):
    count = len(refs) // 2
    sem = refs[-1]
    copies = [pltpu.make_async_copy(refs[i], refs[count + i], sem.at[i]) for i in range(count)]
    for copy in copies:
        copy.start()
    for copy in copies:
        copy.wait()


def body(coupling, incidence, arc_cost, capacity, demand, weights, fleet_slots):
    rows, arcs = coupling.shape
    fleets = fleet_slots.shape[0]
    turns = ROUNDS * ITERS
    f32 = jnp.float32
    hbm = pl.BlockSpec(memory_space=pltpu.HBM)
    dma = pltpu.SemaphoreType.DMA
    outs = [
        jax.ShapeDtypeStruct((1, arcs), f32),
        jax.ShapeDtypeStruct((1, rows // NZ), f32),
        jax.ShapeDtypeStruct((1, fleets), f32),
        jax.ShapeDtypeStruct((1, fleets), f32),
        jax.ShapeDtypeStruct((1, ROUNDS), f32),
    ]
    results = pl.pallas_call(
        kernel,
        out_shape=outs,
        in_specs=[hbm] * 7,
        out_specs=[hbm] * 5,
        scratch_shapes=[
            pltpu.VMEM((1, arcs), f32),
            pltpu.VMEM((1, rows // NZ), f32),
            pltpu.VMEM((1, fleets), f32),
            pltpu.VMEM((1, fleets), f32),
            pltpu.VMEM((1, ROUNDS), f32),
            pltpu.SMEM((arcs // TILE, rows // TILE), jnp.int32),
            pltpu.SMEM((1,), jnp.int32),
            pltpu.VMEM((1, arcs), f32),
            pltpu.VMEM((1, arcs), f32),
            pltpu.VMEM((rows // TILE, TILE), f32),
            pltpu.VMEM((1, fleets), jnp.int32),
            pltpu.VMEM((rows, arcs), jnp.bfloat16),
            pltpu.VMEM((arcs, rows), jnp.bfloat16),
            pltpu.VMEM((arcs, fleets), jnp.bfloat16),
            pltpu.VMEM((turns, NZ, rows // TILE, TILE), f32),
            pltpu.VMEM((SCEN, fleets), f32),
            pltpu.VMEM((ROUNDS, SCEN, fleets), f32),
            pltpu.VMEM((NZ, ROUNDS, fleets), f32),
            pltpu.VMEM((rows // TILE, TILE), f32),
            dma((6 + CHUNKS,)),
            dma((5,)),
            dma((turns,)),
            dma((turns,)),
            dma((2,)),
            dma((2,)),
            dma((ROUNDS,)),
            dma((ROUNDS,)),
            dma,
            dma,
        ],
        compiler_params=pltpu.CompilerParams(
            collective_id=0, has_side_effects=True, vmem_limit_bytes=60 * 1024 * 1024
        ),
        cost_estimate=pl.CostEstimate(
            flops=4 * turns * rows * arcs, bytes_accessed=2 * rows * arcs, transcendentals=0
        ),
    )(
        coupling,
        incidence.T,
        arc_cost.reshape(1, arcs),
        capacity.reshape(1, arcs),
        demand.reshape(rows // TILE, TILE),
        weights,
        fleet_slots.reshape(1, fleets),
    )
    flows, duals, multipliers, consensus, spread = pl.pallas_call(
        place,
        out_shape=outs,
        in_specs=[hbm] * 5,
        out_specs=[hbm] * 5,
        scratch_shapes=[dma((5,))],
    )(*results)
    return flows, duals, multipliers, consensus.reshape(fleets), spread.reshape(ROUNDS)


def solution(mesh):
    in_specs = (
        P(None, "arc"),
        P(None, "arc"),
        P("arc"),
        P("arc"),
        P("scen", None),
        P("scen"),
        P("arc"),
    )
    out_specs = (P("scen", "arc"), P("scen", "arc"), P("scen", "arc"), P("arc"), P())
    return jax.shard_map(body, mesh=mesh, in_specs=in_specs, out_specs=out_specs, check_vma=False)
```

time: 885 us -> 73.9 us (0.08)
  blocking collectives: 841 us -> 0 us
  Pallas kernels: 0 us -> 72.4 us
  other arithmetic: 18.1 us -> 0 us
  local copies, waits for them, and re-layouts: 14.9 us -> 0 us
    psum x3 -> x0, blocking collectives: 661 us -> none  [the longest x2 551 us: weighted_total(): return lax.psum(value, 'scen')]
    unnamed x8 -> x0, blocking collectives: 112 us -> none
    pallas_call x0 -> x2, Pallas kernels: none -> 72.4 us  [the longest x1 71.1 us: body(): pl.pallas_call(kernel, out_shape=outs, in_specs=[hbm] * 7, out_specs=[hbm...]
    all_gather x7 -> x0, blocking collectives: 68.4 us -> none  [body(): lax.all_gather(duals.astype(jnp.bfloat16), 'arc', axis=0, tiled=True)]
    gather x9 -> x0, local copies, waits for them, and re-layouts: 11.5 us -> none  [the longest x7 8.94 us: body(): fleet_push = multipliers + penalty * (flows[fleet_slots] - consensus)]
    scatter-add x8 -> x0, other arithmetic: 11.4 us -> none  [body(): gradient = (arc_cost + dual_pull).at[fleet_slots].add(fleet_push)]
where the time goes in v2:
time: 73.9 us; the launch traced here: 73.7 us
  Pallas kernels  72.4 us (98%)
  between operations  1.29 us (2%)
    pallas_call x1, Pallas kernels, body(): pl.pallas_call(kernel, out_shape=outs, in_specs=[hbm] * 7, out_specs=[hbm...  71.1 us

profile of v2, /device:TPU:1, one launch (start us, length us, event | category | flops | bytes accessed | tf_op | source)
XLA Modules:
  0.0 73.7 jit_solution(603598357425646417)
XLA Ops:
  1.3 71.1 %shard_map.110 = (f32[1,512]{1,0:T(1,128)}, f32[1,128]{1,0:T(1,128)}, f32[1,128]{1,0:T(1,128)}, f32[1,128]{1,0:T(1,128)}, f32[1,2]{1,0:T(1,128)}) custom-call(bf16[1024,512]{1,0:T(8,128)(2,1)} %coupling_hbm.1, s32[4,8]{1,0:T(4,128)} %bitcast.8, f32[1,512]{1,0:T(1,128)} %bitcast.9, f32[1,512]{1,0:T(1,128)} %bitcast.10, f32[8,128]{1,0:T(8,128)} %bitcast.7, ...), custom_call_target="tpu_custom_call" | custom-call | flops 16777216 | bytes 1048576 | tf_op jit(solution)/shard_map/pallas_call | solution.py:315
  72.4 1.3 %shard_map.111 = (f32[1,512]{1,0:T(1,128)}, f32[1,128]{1,0:T(1,128)}, f32[1,128]{1,0:T(1,128)}, f32[1,128]{1,0:T(1,128)}, f32[1,2]{1,0:T(1,128)}) custom-call(f32[1,512]{1,0:T(1,128)} %get-tuple-element.15.refs_0_, f32[1,128]{1,0:T(1,128)} %get-tuple-element.16.refs_1_, f32[1,128]{1,0:T(1,128)} %get-tuple-element.17.refs_2_, ...), custom_call_target="tpu_custom_call" | custom-call | tf_op jit(solution)/shard_map/pallas_call | solution.py:366

commit v3 on v2

--- a/solution.py
+++ b/solution.py
@@ -18,6 +18,7 @@
 NG = NX * NC
 SCEN = NG * NY
 CHUNKS = 4
+EARLY = 26
 NN = (((1,), (0,)), ((), ()))
 NT = (((1,), (1,)), ((), ()))
 
@@ -73,6 +74,8 @@
     masked,
     turned,
     pick,
+    fleet_columns,
+    fleet_rows,
     loads,
     shares,
     fleet,
@@ -101,15 +104,20 @@
         return (other, z)
 
     along_z = [(scen, lax.rem(z + step, NZ)) for step in far(NZ)[:-1]]
-    group = [at(dx, 0, dc) for dx in far(NX) for dc in (1, 0) if dx + dc > 0]
-    plane = [at(0, dy, 0) for dy in far(NY)[:-1]]
+    group_steps = [(dx, 0, dc) for dx in far(NX) for dc in (1, 0) if dx + dc > 0]
+    plane_steps = [(0, dy, 0) for dy in far(NY)[:-1]]
+    group = [at(*step) for step in group_steps]
+    plane = [at(*step) for step in plane_steps]
     steps = [(dx, dy, dc) for dx in range(NX) for dy in range(NY) for dc in range(NC)]
     steps = [s for s in steps if s != (0, 0, 0)]
     steps.sort(key=lambda s: -hops(s[0], NX) - hops(s[1], NY))
 
     barrier = pltpu.get_barrier_semaphore()
-    greeted = along_z + group + plane
-    for other in greeted:
+    greeted = [(hops(step, NZ), other) for step, other in zip(far(NZ), along_z)]
+    greeted += [(hops(step[0], NX), other) for step, other in zip(group_steps, group)]
+    greeted += [(hops(step[1], NY), other) for step, other in zip(plane_steps, plane)]
+    greeted.sort(key=lambda entry: -entry[0])
+    for _, other in greeted:
         pl.semaphore_signal(barrier, inc=1, device_id=other, device_id_type=MESH)
 
     rows, arcs = masked.shape
@@ -198,6 +206,29 @@
     fetch_demand.wait()
     demand = demand_ref[...]
 
+    def gathered(value):
+        return joined(dot(thirds(value), pick[...], NN))
+
+    def on_arcs(value):
+        return joined(dot(thirds(value), pick[...], NT))
+
+    def send_fleet(round_index, some_steps):
+        line = fleet.at[round_index, own_row]
+        for step in some_steps:
+            send(line, line, at(*step), fleet_send.at[round_index], fleet_recv.at[round_index])
+
+    def settle(round_index):
+        arrival = awaited(
+            fleet.at[round_index, pl.ds(0, SCEN - 1)], fleet_send.at[round_index], fleet_recv.at[round_index]
+        )
+        arrival.wait_recv()
+        pending.append(arrival)
+        return jnp.sum(shares[...] * fleet[round_index], axis=0, keepdims=True) / weight_sum
+
+    def deviation(round_index, consensus):
+        gap = fleet[round_index] - consensus
+        return jnp.sum(shares[...] * gap * gap, axis=0, keepdims=True)
+
     def next_duals(duals, turn):
         waits[turn].wait_recv()
         row_load = loads[turn, 0]
@@ -205,41 +236,63 @@
             row_load = row_load + loads[turn, i]
         return jnp.maximum(duals + dual_step * (row_load - demand), 0.0)
 
+    fleet_columns[...] = dot(masked[...], pick[...], NN).astype(jnp.bfloat16)
+    fleet_rows[...] = fleet_columns[...].T
+    fleet_cost = gathered(cost)
+    fleet_capacity = gathered(capacity)
+
+    last_turn = ROUNDS * ITERS - 1
     duals = next_duals(jnp.zeros(demand.shape, jnp.float32), 0)
     multipliers = jnp.zeros((1, fleets), jnp.float32)
+    consensus = jnp.zeros((1, fleets), jnp.float32)
     arc_multipliers = jnp.zeros((1, arcs), jnp.float32)
     arc_consensus = jnp.zeros((1, arcs), jnp.float32)
     deviations = []
     pending = []
     for turn in range(1, ROUNDS * ITERS):
-        row = jnp.concatenate([duals[i : i + 1] for i in range(blocks)], axis=1)
-        gradient = cost + dot(row.astype(jnp.bfloat16), masked[...], NN)
-        push = arc_multipliers + penalty * (flows - arc_consensus)
-        gradient = gradient + jnp.where(is_fleet, push, 0.0)
-        flows_next = jnp.clip(flows - primal_step * gradient, 0.0, capacity)
-        flows_bar = (2.0 * flows_next - flows).astype(jnp.bfloat16)
-        flows = flows_next
         round_index = turn // ITERS
+        row = jnp.concatenate([duals[i : i + 1] for i in range(blocks)], axis=1).astype(jnp.bfloat16)
+        round_starts = turn % ITERS == 0
         round_ends = turn % ITERS == ITERS - 1
+        later = []
+        if round_starts or round_ends:
+            fleet_gradient = fleet_cost + dot(row, fleet_columns[...], NN)
         if round_ends:
-            fleet_flow = joined(dot(thirds(flows), pick[...], NN))
-            heap = fleet.at[round_index]
+            fleet_gradient = fleet_gradient + (multipliers + penalty * (fleet_flow - consensus))
+            fleet_flow = jnp.clip(fleet_flow - primal_step * fleet_gradient, 0.0, fleet_capacity)
             fleet[round_index, own_row, :] = fleet_flow
-            for step in steps:
-                send(
-                    heap.at[own_row],
-                    heap.at[own_row],
-                    at(*step),
-                    fleet_send.at[round_index],
-                    fleet_recv.at[round_index],
-                )
-            arrival = awaited(
-                heap.at[pl.ds(0, SCEN - 1)], fleet_send.at[round_index], fleet_recv.at[round_index]
-            )
-        load = dot(flows_bar, turned[...], NN)
+            early = len(steps) if turn == last_turn else EARLY
+            send_fleet(round_index, steps[:early])
+            later = steps[early:]
+        gradient = cost + dot(row, masked[...], NN)
+        if round_starts:
+            flows_next = jnp.clip(flows - primal_step * gradient, 0.0, capacity)
+            flows_bar = jnp.where(is_fleet, 0.0, 2.0 * flows_next - flows).astype(jnp.bfloat16)
+            load = dot(flows_bar, turned[...], NN)
+            consensus = settle(round_index - 1)
+            multipliers = multipliers + penalty * (fleet_flow - consensus)
+            fleet_gradient = fleet_gradient + (multipliers + penalty * (fleet_flow - consensus))
+            fleet_next = jnp.clip(fleet_flow - primal_step * fleet_gradient, 0.0, fleet_capacity)
+            fleet_bar = (2.0 * fleet_next - fleet_flow).astype(jnp.bfloat16)
+            load = load + dot(fleet_bar, fleet_rows[...], NN)
+        else:
+            push = arc_multipliers + penalty * (flows - arc_consensus)
+            gradient = gradient + jnp.where(is_fleet, push, 0.0)
+            flows_next = jnp.clip(flows - primal_step * gradient, 0.0, capacity)
+            flows_bar = (2.0 * flows_next - flows).astype(jnp.bfloat16)
+            load = dot(flows_bar, turned[...], NN)
         for i in range(blocks):
             loads[turn, z, i : i + 1, :] = load[:, i * TILE : (i + 1) * TILE]
         waits.append(exchange(loads.at[turn], load_send.at[turn], load_recv.at[turn]))
+        send_fleet(round_index, later)
+        if round_starts:
+            flows_next = jnp.where(is_fleet, on_arcs(fleet_next), flows_next)
+            arc_consensus = on_arcs(consensus)
+            arc_multipliers = on_arcs(multipliers)
+            deviations.append(deviation(round_index - 1, consensus))
+        flows = flows_next
+        if turn % ITERS == ITERS - 2:
+            fleet_flow = gathered(flows)
         if turn == 1:
             share_group.wait_recv()
             own_rows = pl.ds(pl.multiple_of(y * NG, NG), NG)
@@ -250,29 +303,24 @@
             share_plane.wait_recv()
             pending += [share_group, share_plane]
             weight_sum = jnp.sum(shares[...], axis=0, keepdims=True)
-        duals = next_duals(duals, turn)
-        if round_ends:
-            if turn == ROUNDS * ITERS - 1:
-                flows_ref[...] = flows
-                all_duals[...] = duals
-                duals_ref[...] = all_duals[pl.ds(z, 1), :]
-                stores = [store(0, flows_ref, flows_out), store(1, duals_ref, duals_out)]
-            arrival.wait_recv()
-            pending.append(arrival)
-            all_fleet = heap[...]
-            consensus = jnp.sum(shares[...] * all_fleet, axis=0, keepdims=True) / weight_sum
-            gap = all_fleet - consensus
-            deviations.append(jnp.sum(shares[...] * gap * gap, axis=0, keepdims=True))
-            multipliers = multipliers + penalty * (fleet_flow - consensus)
-            if turn < ROUNDS * ITERS - 1:
-                arc_consensus = joined(dot(thirds(consensus), pick[...], NT))
-                arc_multipliers = arc_multipliers + penalty * jnp.where(is_fleet, flows - arc_consensus, 0.0)
-
+        if turn < last_turn:
+            duals = next_duals(duals, turn)
+
+    consensus = settle(ROUNDS - 1)
+    deviations.append(deviation(ROUNDS - 1, consensus))
     squares[z] = jnp.concatenate(deviations, axis=0)
     wait = exchange(squares, square_send, square_recv)
-    multipliers_ref[...] = multipliers
+    multipliers_ref[...] = multipliers + penalty * (fleet_flow - consensus)
     consensus_ref[...] = consensus
-    stores += [store(2, multipliers_ref, multipliers_out), store(3, consensus_ref, consensus_out)]
+    flows_ref[...] = flows
+    all_duals[...] = next_duals(duals, last_turn)
+    duals_ref[...] = all_duals[pl.ds(z, 1), :]
+    stores = [
+        store(0, flows_ref, flows_out),
+        store(1, duals_ref, duals_out),
+        store(2, multipliers_ref, multipliers_out),
+        store(3, consensus_ref, consensus_out),
+    ]
     for done in waits + pending:
         done.wait_send()
     wait.wait_recv()
@@ -332,6 +380,8 @@
             pltpu.VMEM((rows, arcs), jnp.bfloat16),
             pltpu.VMEM((arcs, rows), jnp.bfloat16),
             pltpu.VMEM((arcs, fleets), jnp.bfloat16),
+            pltpu.VMEM((rows, fleets), jnp.bfloat16),
+            pltpu.VMEM((fleets, rows), jnp.bfloat16),
             pltpu.VMEM((turns, NZ, rows // TILE, TILE), f32),
             pltpu.VMEM((SCEN, fleets), f32),
             pltpu.VMEM((ROUNDS, SCEN, fleets), f32),

time: 73.9 us -> 73.3 us (level)
  no operation moved by 1% of the time
where the time goes in v3:
time: 73.3 us; the launch traced here: 73.1 us
  Pallas kernels  71.9 us (98%)
  between operations  1.29 us (2%)
    pallas_call x1, Pallas kernels, body(): pl.pallas_call(kernel, out_shape=outs, in_specs=[hbm] * 7, out_specs=[hbm...  70.6 us

profile of v3, /device:TPU:1, one launch (start us, length us, event | category | flops | bytes accessed | tf_op | source)
XLA Modules:
  0.0 73.1 jit_solution(11595021205278148430)
XLA Ops:
  1.3 70.6 %shard_map.110 = (f32[1,512]{1,0:T(1,128)}, f32[1,128]{1,0:T(1,128)}, f32[1,128]{1,0:T(1,128)}, f32[1,128]{1,0:T(1,128)}, f32[1,2]{1,0:T(1,128)}) custom-call(bf16[1024,512]{1,0:T(8,128)(2,1)} %coupling_hbm.1, s32[4,8]{1,0:T(4,128)} %bitcast.8, f32[1,512]{1,0:T(1,128)} %bitcast.9, f32[1,512]{1,0:T(1,128)} %bitcast.10, f32[8,128]{1,0:T(8,128)} %bitcast.7, ...), custom_call_target="tpu_custom_call" | custom-call | flops 16777216 | bytes 1048576 | tf_op jit(solution)/shard_map/pallas_call | solution.py:363
  71.9 1.3 %shard_map.111 = (f32[1,512]{1,0:T(1,128)}, f32[1,128]{1,0:T(1,128)}, f32[1,128]{1,0:T(1,128)}, f32[1,128]{1,0:T(1,128)}, f32[1,2]{1,0:T(1,128)}) custom-call(f32[1,512]{1,0:T(1,128)} %get-tuple-element.15.refs_0_, f32[1,128]{1,0:T(1,128)} %get-tuple-element.16.refs_1_, f32[1,128]{1,0:T(1,128)} %get-tuple-element.17.refs_2_, ...), custom_call_target="tpu_custom_call" | custom-call | tf_op jit(solution)/shard_map/pallas_call | solution.py:416

commit v4 on v3

--- a/solution.py
+++ b/solution.py
@@ -19,6 +19,7 @@
 SCEN = NG * NY
 CHUNKS = 4
 EARLY = 26
+FIRST = 4
 NN = (((1,), (0,)), ((), ()))
 NT = (((1,), (1,)), ((), ()))
 
@@ -59,12 +60,14 @@
     duals_out,
     multipliers_out,
     consensus_out,
-    spread_out,
+    squares_out,
+    weight_out,
     flows_ref,
     duals_ref,
     multipliers_ref,
     consensus_ref,
-    spread_ref,
+    squares_ref,
+    weight_ref,
     incidence,
     weights,
     cost_ref,
@@ -79,7 +82,6 @@
     loads,
     shares,
     fleet,
-    squares,
     all_duals,
     fetch_sem,
     store_sem,
@@ -117,9 +119,12 @@
     greeted += [(hops(step[0], NX), other) for step, other in zip(group_steps, group)]
     greeted += [(hops(step[1], NY), other) for step, other in zip(plane_steps, plane)]
     greeted.sort(key=lambda entry: -entry[0])
-    for _, other in greeted:
-        pl.semaphore_signal(barrier, inc=1, device_id=other, device_id_type=MESH)
-
+
+    def greet(some):
+        for _, other in some:
+            pl.semaphore_signal(barrier, inc=1, device_id=other, device_id_type=MESH)
+
+    greet(greeted[:FIRST])
     rows, arcs = masked.shape
     blocks = rows // TILE
     fleets = slots_ref.shape[1]
@@ -137,6 +142,7 @@
     fetch_capacity = fetch(capacity_hbm, capacity_ref)
     parts = [pl.ds(chunk * depth, depth) for chunk in range(CHUNKS)]
     fetch_masked = [fetch(coupling_hbm.at[part], masked.at[part]) for part in parts]
+    greet(greeted[FIRST:])
     fetch_slots = fetch(slots_hbm, slots_ref)
     fetch_demand = fetch(demand_hbm, demand_ref)
     fetch_weights = fetch(weights_hbm, weights)
@@ -303,19 +309,24 @@
             share_plane.wait_recv()
             pending += [share_group, share_plane]
             weight_sum = jnp.sum(shares[...], axis=0, keepdims=True)
+            weight_ref[...] = weight_sum
+            stores = [store(5, weight_ref, weight_out)]
         if turn < last_turn:
             duals = next_duals(duals, turn)
 
     consensus = settle(ROUNDS - 1)
     deviations.append(deviation(ROUNDS - 1, consensus))
-    squares[z] = jnp.concatenate(deviations, axis=0)
-    wait = exchange(squares, square_send, square_recv)
+    squares_ref[...] = jnp.concatenate(deviations, axis=0)
+    for partner in along_z:
+        send(squares_ref, squares_out.at[z], partner, square_send, square_recv)
+    wait = awaited(squares_out.at[pl.ds(0, NZ - 1)], square_send, square_recv)
     multipliers_ref[...] = multipliers + penalty * (fleet_flow - consensus)
     consensus_ref[...] = consensus
     flows_ref[...] = flows
     all_duals[...] = next_duals(duals, last_turn)
     duals_ref[...] = all_duals[pl.ds(z, 1), :]
-    stores = [
+    stores += [
+        store(4, squares_ref, squares_out.at[z]),
         store(0, flows_ref, flows_out),
         store(1, duals_ref, duals_out),
         store(2, multipliers_ref, multipliers_out),
@@ -323,27 +334,53 @@
     ]
     for done in waits + pending:
         done.wait_send()
-    wait.wait_recv()
-    total = squares[0]
-    for i in range(1, NZ):
-        total = total + squares[i]
-    total = jnp.sum(total, axis=1, keepdims=True)
-    spread = jnp.sqrt(total / (weight_sum[:, 0:1] * (fleets * NZ)) + 1e-06)
-    spread_ref[...] = jnp.concatenate([spread[i : i + 1] for i in range(ROUNDS)], axis=1)
-    stores.append(store(4, spread_ref, spread_out))
-    wait.wait_send()
     for done in stores:
         done.wait()
-
-
-def place(*refs):
-    count = len(refs) // 2
-    sem = refs[-1]
-    copies = [pltpu.make_async_copy(refs[i], refs[count + i], sem.at[i]) for i in range(count)]
+    wait.wait()
+
+
+def place(
+    flows,
+    duals,
+    multipliers,
+    consensus,
+    squares,
+    weight,
+    flows_out,
+    duals_out,
+    multipliers_out,
+    consensus_out,
+    spread_out,
+    squares_ref,
+    weight_ref,
+    spread_ref,
+    sem,
+):
+    pairs = [
+        (squares, squares_ref),
+        (weight, weight_ref),
+        (flows, flows_out),
+        (duals, duals_out),
+        (multipliers, multipliers_out),
+        (consensus, consensus_out),
+    ]
+    copies = [pltpu.make_async_copy(*pair, sem.at[i]) for i, pair in enumerate(pairs)]
     for copy in copies:
         copy.start()
-    for copy in copies:
+    copies[0].wait()
+    copies[1].wait()
+    total = squares_ref[0]
+    for i in range(1, NZ):
+        total = total + squares_ref[i]
+    total = jnp.sum(total, axis=1, keepdims=True)
+    fleets = weight_ref.shape[1]
+    spread = jnp.sqrt(total / (weight_ref[:, 0:1] * (fleets * NZ)) + 1e-06)
+    spread_ref[...] = jnp.concatenate([spread[i : i + 1] for i in range(ROUNDS)], axis=1)
+    last = pltpu.make_async_copy(spread_ref, spread_out, sem.at[len(pairs)])
+    last.start()
+    for copy in copies[2:]:
         copy.wait()
+    last.wait()
 
 
 def body(coupling, incidence, arc_cost, capacity, demand, weights, fleet_slots):
@@ -358,19 +395,22 @@
         jax.ShapeDtypeStruct((1, rows // NZ), f32),
         jax.ShapeDtypeStruct((1, fleets), f32),
         jax.ShapeDtypeStruct((1, fleets), f32),
-        jax.ShapeDtypeStruct((1, ROUNDS), f32),
     ]
+    squares = jax.ShapeDtypeStruct((NZ, ROUNDS, fleets), f32)
+    weight = jax.ShapeDtypeStruct((1, fleets), f32)
+    spread = jax.ShapeDtypeStruct((1, ROUNDS), f32)
     results = pl.pallas_call(
         kernel,
-        out_shape=outs,
+        out_shape=outs + [squares, weight],
         in_specs=[hbm] * 7,
-        out_specs=[hbm] * 5,
+        out_specs=[hbm] * 6,
         scratch_shapes=[
             pltpu.VMEM((1, arcs), f32),
             pltpu.VMEM((1, rows // NZ), f32),
             pltpu.VMEM((1, fleets), f32),
             pltpu.VMEM((1, fleets), f32),
-            pltpu.VMEM((1, ROUNDS), f32),
+            pltpu.VMEM((ROUNDS, fleets), f32),
+            pltpu.VMEM((1, fleets), f32),
             pltpu.SMEM((arcs // TILE, rows // TILE), jnp.int32),
             pltpu.SMEM((1,), jnp.int32),
             pltpu.VMEM((1, arcs), f32),
@@ -385,10 +425,9 @@
             pltpu.VMEM((turns, NZ, rows // TILE, TILE), f32),
             pltpu.VMEM((SCEN, fleets), f32),
             pltpu.VMEM((ROUNDS, SCEN, fleets), f32),
-            pltpu.VMEM((NZ, ROUNDS, fleets), f32),
             pltpu.VMEM((rows // TILE, TILE), f32),
             dma((6 + CHUNKS,)),
-            dma((5,)),
+            dma((6,)),
             dma((turns,)),
             dma((turns,)),
             dma((2,)),
@@ -415,10 +454,15 @@
     )
     flows, duals, multipliers, consensus, spread = pl.pallas_call(
         place,
-        out_shape=outs,
-        in_specs=[hbm] * 5,
+        out_shape=outs + [spread],
+        in_specs=[hbm] * 6,
         out_specs=[hbm] * 5,
-        scratch_shapes=[dma((5,))],
+        scratch_shapes=[
+            pltpu.VMEM(squares.shape, f32),
+            pltpu.VMEM(weight.shape, f32),
+            pltpu.VMEM(spread.shape, f32),
+            dma((7,)),
+        ],
     )(*results)
     return flows, duals, multipliers, consensus.reshape(fleets), spread.reshape(ROUNDS)
 

time: 73.3 us -> 73 us (level)
  no operation moved by 1% of the time
where the time goes in v4:
time: 73 us; the launch traced here: 72.8 us
  Pallas kernels  71.5 us (98%)
  between operations  1.29 us (2%)
    pallas_call x1, Pallas kernels, body(): pl.pallas_call(kernel, out_shape=outs + [squares, weight], in_specs=[hbm]...  70 us

profile of v4, /device:TPU:1, one launch (start us, length us, event | category | flops | bytes accessed | tf_op | source)
XLA Modules:
  0.0 72.8 jit_solution(8059492768835755215)
XLA Ops:
  1.3 70.0 %shard_map.110 = (f32[1,512]{1,0:T(1,128)}, f32[1,128]{1,0:T(1,128)}, f32[1,128]{1,0:T(1,128)}, f32[1,128]{1,0:T(1,128)}, f32[8,2,128]{2,1,0:T(2,128)}, /*index=5*/f32[1,128]{1,0:T(1,128)}) custom-call(bf16[1024,512]{1,0:T(8,128)(2,1)} %coupling_hbm.1, s32[4,8]{1,0:T(4,128)} %bitcast.8, f32[1,512]{1,0:T(1,128)} %bitcast.9, f32[1,512]{1,0:T(1,128)} %bitcast.10, ...), custom_call_target="tpu_custom_call" | custom-call | flops 16777216 | bytes 1048576 | tf_op jit(solution)/shard_map/pallas_call | solution.py:402
  71.3 1.4 %shard_map.111 = (f32[1,512]{1,0:T(1,128)}, f32[1,128]{1,0:T(1,128)}, f32[1,128]{1,0:T(1,128)}, f32[1,128]{1,0:T(1,128)}, f32[1,2]{1,0:T(1,128)}) custom-call(f32[1,512]{1,0:T(1,128)} %get-tuple-element.16.flows, f32[1,128]{1,0:T(1,128)} %get-tuple-element.17.duals, f32[1,128]{1,0:T(1,128)} %get-tuple-element.18.multipliers, ...), custom_call_target="tpu_custom_call" | custom-call | tf_op jit(solution)/shard_map/pallas_call | solution.py:455
